TPU v7x, 128 devices: a whole 4x4x4 slice. The times are simulated.
128 devices in a mesh: band: 4 (over x_lo, core), slab: 32 (over x_hi, z, y).
Axes of the slice: x: 4 (x_hi: 2, x_lo: 2; x = x_hi * 2 + x_lo), y: 4, z: 4, core: 2. Of those that a mesh axis runs over, the one named last changes fastest.
Arguments:
- resident: float32 [8, 128, 128, 128], P('band', 'slab'), may hold values from -5 to 5
- blocks: float32 [16, 128, 128, 128], P('band', 'slab'), may hold values from -5 to 5
- occupation: float32 [16], replicated, may hold values from 0.25 to 1
Outputs:
- exchange_term: float32 [8, 128, 128, 128], P('band', 'slab')
All inputs are finite; a program needn't handle non-finite values.
Results may differ from a plain program's by a relative error of at most 0.0001.
Values sent between devices are 32-bit elements; how exact they have to be, the bound alone decides.
A program may use at most 128 MiB of HBM per device.

v0:
```python
import math
import jax
import jax.numpy as jnp
from jax import lax
from jax.sharding import PartitionSpec as P

KAPPA_SQ = 0.01


def dft_tables(grid_len):
    indices = jnp.arange(grid_len, dtype=jnp.int32)
    product = indices[:, None] * indices[None, :] % grid_len
    angles = product.astype(jnp.float32) * (2.0 * math.pi / grid_len)
    return (jnp.cos(angles), jnp.sin(angles))


def transform(real_part, imag_part, form, cos_t, sin_t, sign_val):

    def apply(values, table):
        return jnp.einsum(
            form, values, table, precision=lax.Precision.HIGHEST, preferred_element_type=jnp.float32
        )

    real_cos = apply(real_part, cos_t)
    real_sin = apply(real_part, sin_t)
    imag_cos = apply(imag_part, cos_t)
    imag_sin = apply(imag_part, sin_t)
    return (real_cos - sign_val * imag_sin, imag_cos + sign_val * real_sin)


def wave_of(indices, grid_len):
    signed = jnp.where(indices > (grid_len - 1) // 2, indices - grid_len, indices)
    return signed.astype(jnp.float32) * (2.0 * math.pi / grid_len)


def coulomb(wave_z, wave_y, wave_x):
    squared = wave_z[:, None, None] ** 2 + wave_y[None, :, None] ** 2 + wave_x[None, None, :] ** 2
    return 4.0 * math.pi / (squared + KAPPA_SQ)


def per_device(resident, blocks, occupation):
    orb_count, plane_count, grid_len, _ = resident.shape
    local_src = blocks.shape[0]
    group_count = lax.axis_size("band")
    src_count = local_src * group_count
    cos_t, sin_t = dft_tables(grid_len)
    along_x = "fzyx,xk->fzyk"
    along_y = "fzyx,yk->fzkx"
    along_z = "fzyx,zk->fkyx"
    source = lax.all_gather(blocks, "band", axis=0, tiled=True)
    count_pairs = source.shape[0] // 2
    even_src = source[0::2]
    odd_src = source[1::2]
    real_part = (resident[:, None] * even_src[None]).reshape(
        orb_count * count_pairs, plane_count, grid_len, grid_len
    )
    imag_part = (resident[:, None] * odd_src[None]).reshape(
        orb_count * count_pairs, plane_count, grid_len, grid_len
    )
    real_part, imag_part = transform(real_part, imag_part, along_x, cos_t, sin_t, -1.0)
    real_part, imag_part = transform(real_part, imag_part, along_y, cos_t, sin_t, -1.0)
    shaped = (orb_count, count_pairs, plane_count, grid_len, grid_len)
    real_part, imag_part = (real_part.reshape(shaped), imag_part.reshape(shaped))
    field_count = orb_count * (src_count // 2)
    flat = (field_count, plane_count, grid_len, grid_len)
    real_part = real_part.reshape(flat)
    imag_part = imag_part.reshape(flat)
    all_waves = wave_of(jnp.arange(grid_len, dtype=jnp.int32), grid_len)
    position = lax.axis_index("slab")
    col_real = lax.all_to_all(real_part, "slab", split_axis=2, concat_axis=1, tiled=True)
    col_imag = lax.all_to_all(imag_part, "slab", split_axis=2, concat_axis=1, tiled=True)
    width_y = col_real.shape[2]
    local_waves = wave_of(position * width_y + jnp.arange(width_y, dtype=jnp.int32), grid_len)
    kernel = coulomb(all_waves, local_waves, all_waves)
    col_real, col_imag = transform(col_real, col_imag, along_z, cos_t, sin_t, -1.0)
    col_real = col_real * kernel[None]
    col_imag = col_imag * kernel[None]
    col_real, col_imag = transform(col_real, col_imag, along_z, cos_t, sin_t, 1.0)
    real_part = lax.all_to_all(col_real, "slab", split_axis=1, concat_axis=2, tiled=True)
    imag_part = lax.all_to_all(col_imag, "slab", split_axis=1, concat_axis=2, tiled=True)
    real_part, imag_part = transform(real_part, imag_part, along_y, cos_t, sin_t, 1.0)
    real_part, imag_part = transform(real_part, imag_part, along_x, cos_t, sin_t, 1.0)
    scale_inv = 1.0 / float(grid_len * grid_len * grid_len)
    shaped = (orb_count, src_count // 2, plane_count, grid_len, grid_len)
    pot_even = real_part.reshape(shaped) * scale_inv
    pot_odd = imag_part.reshape(shaped) * scale_inv
    weighted_even = source[0::2] * occupation[0::2][:, None, None, None]
    weighted_odd = source[1::2] * occupation[1::2][:, None, None, None]
    summed = jnp.sum(pot_even * weighted_even[None], axis=1) + jnp.sum(
        pot_odd * weighted_odd[None], axis=1
    )
    return -summed


def solution(mesh):
    placed = (P("band", "slab", None, None), P("band", "slab", None, None), P())
    return jax.shard_map(
        per_device,
        mesh=mesh,
        in_specs=placed,
        out_specs=P("band", "slab", None, None),
        check_vma=False,
    )
```

profile of v0, /device:TPU:6, one launch (start us, length us, event | category | flops | bytes accessed | tf_op | source)
XLA Modules:
  0.0 448.1 jit_solution(13577813756343298961)
XLA Ops:
  6.5 0.0 all-gather.2.cloned.1.call-start
  6.5 0.7 all-gather.2.cloned.1.call-update
  7.3 0.7 slice.17
  8.0 0.7 slice.16
  8.8 48.0 %all-gather.2.cloned.1.call-done = f32[16,4,128,128]{3,2,1,0:T(8,128)} async-done(((f32[4,4,128,128]{3,2,1,0:T(8,128)}), f32[16,4,128,128]{3,2,1,0:T(8,128)}) %all-gather.2.cloned.1.call-update) | async-done | bytes 4194320 | tf_op jit(solution)/shard_map/all_gather | solution.py:50
  56.7 4.7 %multiply_multiply_fusion = (f32[8,4,128,128]{3,2,1,0:T(8,128)}, f32[8,4,128,128]{3,2,1,0:T(8,128)S(1)}, f32[8,4,128,128]{3,2,1,0:T(8,128)S(1)}, f32[8,4,128,128]{3,2,1,0:T(8,128)S(1)}) fusion(f32[8]{0:T(128)S(1)} %slice.17, f32[16,4,128,128]{3,2,1,0:T(8,128)} %all-gather.2.cloned.1.call-done, f32[8]{0:T(128)S(1)} %slice.16), kind=kLoop, calls=%fused_computation.30 | loop fusion | flops 2097152 | bytes 12582976 | tf_op jit(solution)/shard_map/mul | solution.py:90
  61.5 0.0 copy-done.9
  61.5 1.4 broadcast_multiply_fusion.1
  62.9 3.8 fusion.50
  66.7 3.7 fusion.52
  70.3 4.1 multiply_add_fusion
  74.5 0.0 copy-start.2
  74.5 3.8 multiply_subtract_fusion
  78.3 0.0 copy-start.3
  78.3 4.3 fusion.54
  82.6 0.0 copy-done.2
  82.6 0.0 copy-done.3
  82.7 15.0 %subtract_bitcast_fusion.1 = f32[16,4,128,128]{3,2,1,0:T(8,128)S(1)} fusion(f32[128,16,4,128]{3,0,2,1:T(8,128)S(1)} %fusion.54, f32[16,4,128,128]{3,2,1,0:T(8,128)S(1)} %multiply_add_fusion), kind=kOutput, calls=%fused_computation.23 | convolution fusion | flops 1612939264 | bytes 12582912 | tf_op jit(solution)/shard_map/fzyx,yk->fzkx/dot_general | solution.py:20
  97.6 4.7 %copy.26 = f32[16,4,128,128]{3,1,0,2:T(4,128)} copy(f32[16,4,128,128]{3,2,1,0:T(8,128)S(1)} %subtract_bitcast_fusion.1) | data formatting | bytes 8388608 | tf_op jit(solution)/shard_map/sub | solution.py:28
  102.3 10.1 %all-to-all-start = ((f32[16,4,128,128]{3,1,0,2:T(4,128)}), f32[16,4,128,128]{3,1,0,2:T(4,128)}, u32[]{:S(2)}, u32[]{:S(2)}) async-start(f32[16,4,128,128]{3,1,0,2:T(4,128)} %copy.26), calls=%async_computation | async-start | bytes 8388608 | tf_op jit(solution)/shard_map/all_to_all | solution.py:70
  112.4 0.0 copy-start.4
  112.4 6.1 %fusion.46 = f32[128,16,4,128]{3,0,2,1:T(8,128)S(1)} fusion(f32[16,4,128,128]{3,2,1,0:T(8,128)} %copy-done.2), kind=kOutput, calls=%fused_computation.59 | convolution fusion | flops 1610842112 | bytes 8388608 | tf_op jit(solution)/shard_map/fzyx,yk->fzkx/dot_general | solution.py:20
  118.4 0.0 copy-done.4
  118.5 4.3 add_bitcast_fusion.1
  122.8 4.7 %copy.31 = f32[16,4,128,128]{3,1,0,2:T(4,128)} copy(f32[16,4,128,128]{3,2,1,0:T(8,128)S(1)} %add_bitcast_fusion.1) | data formatting | bytes 8388608 | tf_op jit(solution)/shard_map/add | solution.py:28
  127.4 43.5 %all-to-all-done = f32[16,4,128,128]{3,1,0,2:T(4,128)} async-done(((f32[16,4,128,128]{3,1,0,2:T(4,128)}), f32[16,4,128,128]{3,1,0,2:T(4,128)}, u32[]{:S(2)}, u32[]{:S(2)}) %all-to-all-start) | async-done | bytes 4194336 | tf_op jit(solution)/shard_map/all_to_all | solution.py:70
  170.9 13.0 %all-to-all-start.1 = ((f32[16,4,128,128]{3,1,0,2:T(4,128)}), f32[16,4,128,128]{3,1,0,2:T(4,128)}, u32[]{:S(2)}, u32[]{:S(2)}) async-start(f32[16,4,128,128]{3,1,0,2:T(4,128)} %copy.31), calls=%async_computation.1 | async-start | bytes 8388608 | tf_op jit(solution)/shard_map/all_to_all | solution.py:71
  183.9 0.1 broadcast_add_fusion
  184.0 0.1 add_divide_fusion
  184.2 5.3 %copy.27 = f32[16,4,32,4,128]{4,1,2,3,0:T(4,128)} copy(f32[16,4,32,4,128]{4,1,0,3,2:T(4,128)} %bitcast.14) | data formatting | bytes 8388608 | tf_op jit(solution)/shard_map/all_to_all | solution.py:70
  189.5 49.6 %all-to-all-done.1 = f32[16,4,128,128]{3,1,0,2:T(4,128)} async-done(((f32[16,4,128,128]{3,1,0,2:T(4,128)}), f32[16,4,128,128]{3,1,0,2:T(4,128)}, u32[]{:S(2)}, u32[]{:S(2)}) %all-to-all-start.1) | async-done | bytes 4194336 | tf_op jit(solution)/shard_map/all_to_all | solution.py:71
  239.1 3.4 copy.32
  242.5 0.0 copy-start.6
  242.5 4.3 fusion.44
  246.8 0.0 copy-done.6
  246.8 4.3 fusion.56
  251.1 5.2 %add_multiply_fusion = f32[128,16,4,128]{3,0,2,1:T(8,128)S(1)} fusion(f32[128,16,4,128]{3,0,2,1:T(8,128)S(1)} %fusion.44, f32[16,128,4,128]{3,1,2,0:T(8,128)S(1)} %bitcast.157, f32[128,4,128]{2,0,1:T(8,128)S(1)} %add_divide_fusion), kind=kOutput, calls=%fused_computation.20 | convolution fusion | flops 1613987840 | bytes 12845056 | tf_op jit(solution)/shard_map/fzyx,zk->fkyx/dot_general | solution.py:20
  256.3 0.0 copy-start.5
  256.3 4.8 %subtract_multiply_fusion = f32[128,16,4,128]{3,0,2,1:T(8,128)S(1)} fusion(f32[128,16,4,128]{3,0,2,1:T(8,128)S(1)} %fusion.56, f32[16,128,4,128]{3,1,2,0:T(8,128)S(1)} %bitcast.163, f32[128,4,128]{2,0,1:T(8,128)S(1)} %add_divide_fusion), kind=kOutput, calls=%fused_computation.21 | convolution fusion | flops 1613987840 | bytes 12845056 | tf_op jit(solution)/shard_map/fzyx,zk->fkyx/dot_general | solution.py:20
  261.1 0.0 copy-done.5
  261.1 0.0 copy-start
  261.1 4.3 fusion.10
  265.5 0.0 copy-done
  265.5 4.8 %subtract_bitcast_fusion = f32[16,128,4,128]{3,1,2,0:T(8,128)S(1)} fusion(f32[128,16,4,128]{3,0,2,1:T(8,128)S(1)} %fusion.10, f32[128,16,4,128]{3,0,2,1:T(8,128)S(1)} %subtract_multiply_fusion), kind=kOutput, calls=%fused_computation.19 | convolution fusion | flops 1611890688 | bytes 12582912 | tf_op jit(solution)/shard_map/fzyx,zk->fkyx/dot_general | solution.py:20
  270.2 4.7 %copy.38 = f32[16,128,4,128]{3,2,0,1:T(4,128)} copy(f32[16,128,4,128]{3,1,2,0:T(8,128)S(1)} %subtract_bitcast_fusion) | data formatting | bytes 8388608 | tf_op jit(solution)/shard_map/sub | solution.py:28
  274.9 8.8 %all-to-all-start.2 = ((f32[16,128,4,128]{3,2,0,1:T(4,128)}), f32[16,128,4,128]{3,2,0,1:T(4,128)}, u32[]{:S(2)}, u32[]{:S(2)}) async-start(f32[16,128,4,128]{3,2,0,1:T(4,128)} %copy.38), calls=%async_computation.2 | async-start | bytes 8388608 | tf_op jit(solution)/shard_map/all_to_all | solution.py:79
  283.7 0.0 copy-start.1
  283.7 6.1 %fusion.8 = f32[128,16,4,128]{3,0,2,1:T(8,128)S(1)} fusion(f32[128,16,4,128]{3,0,2,1:T(8,128)} %copy-done.5), kind=kOutput, calls=%fused_computation.8 | convolution fusion | flops 1610842112 | bytes 8388608 | tf_op jit(solution)/shard_map/fzyx,zk->fkyx/dot_general | solution.py:20
  289.8 4.1 add_bitcast_fusion
  293.8 4.7 %copy.43 = f32[16,128,4,128]{3,2,0,1:T(4,128)} copy(f32[16,128,4,128]{3,1,2,0:T(8,128)S(1)} %add_bitcast_fusion) | data formatting | bytes 8388608 | tf_op jit(solution)/shard_map/add | solution.py:28
  298.5 38.6 %all-to-all-done.2 = f32[16,128,4,128]{3,2,0,1:T(4,128)} async-done(((f32[16,128,4,128]{3,2,0,1:T(4,128)}), f32[16,128,4,128]{3,2,0,1:T(4,128)}, u32[]{:S(2)}, u32[]{:S(2)}) %all-to-all-start.2) | async-done | bytes 4194336 | tf_op jit(solution)/shard_map/all_to_all | solution.py:79
  337.2 7.5 %all-to-all-start.3 = ((f32[16,128,4,128]{3,2,0,1:T(4,128)}), f32[16,128,4,128]{3,2,0,1:T(4,128)}, u32[]{:S(2)}, u32[]{:S(2)}) async-start(f32[16,128,4,128]{3,2,0,1:T(4,128)} %copy.43), calls=%async_computation.3 | async-start | bytes 8388608 | tf_op jit(solution)/shard_map/all_to_all | solution.py:80
  344.7 5.3 %copy.39 = f32[16,32,4,4,128]{4,3,1,2,0:T(4,128)} copy(f32[16,32,4,4,128]{4,3,0,2,1:T(4,128)} %bitcast.32) | data formatting | bytes 8388608 | tf_op jit(solution)/shard_map/all_to_all | solution.py:79
  350.0 52.2 %all-to-all-done.3 = f32[16,128,4,128]{3,2,0,1:T(4,128)} async-done(((f32[16,128,4,128]{3,2,0,1:T(4,128)}), f32[16,128,4,128]{3,2,0,1:T(4,128)}, u32[]{:S(2)}, u32[]{:S(2)}) %all-to-all-start.3) | async-done | bytes 4194336 | tf_op jit(solution)/shard_map/all_to_all | solution.py:80
  402.2 3.4 copy.44
  405.6 4.3 fusion.41
  409.9 4.3 fusion.59
  414.2 4.6 %convolution_add_fusion = f32[128,16,4,128]{3,0,2,1:T(8,128)S(1)} fusion(f32[128,16,4,128]{3,0,2,1:T(8,128)S(1)} %fusion.41, f32[16,4,128,128]{3,2,1,0:T(8,128)S(1)} %bitcast.159), kind=kOutput, calls=%fused_computation.28 | convolution fusion | flops 1611890688 | bytes 12582912 | tf_op jit(solution)/shard_map/fzyx,yk->fzkx/dot_general | solution.py:20
  418.8 3.8 fusion
  422.6 3.8 fusion.2
  426.5 4.7 %convolution_subtract_fusion = f32[128,16,4,128]{3,0,2,1:T(8,128)S(1)} fusion(f32[128,16,4,128]{3,0,2,1:T(8,128)S(1)} %fusion.59, f32[16,4,128,128]{3,2,1,0:T(8,128)S(1)} %bitcast.161), kind=kOutput, calls=%fused_computation.29 | convolution fusion | flops 1611890688 | bytes 12582912 | tf_op jit(solution)/shard_map/fzyx,yk->fzkx/dot_general | solution.py:20
  431.2 4.4 multiply_reduce_fusion
  435.6 4.4 multiply_reduce_fusion.1
  439.9 0.9 add_negate_fusion
  (8 shorter events, 0.0 us)
Async XLA Ops:
  6.5 50.2 %all-gather.2.cloned.1.call-start = ((), (), s32[]{:S(2)}) async-start(), calls=%async_computation.4 | async-start | bytes 5242880 | tf_op jit(solution)/shard_map/all_gather | solution.py:50
  8.7 52.7 %copy-start.9 = (f32[2,4,128,128]{3,2,1,0:T(8,128)S(1)}, f32[2,4,128,128]{3,2,1,0:T(8,128)}, u32[]{:S(2)}) copy-start(f32[2,4,128,128]{3,2,1,0:T(8,128)} %param.3) | copy-start | bytes 1572868
  74.5 8.2 %copy-start.2 = (f32[16,4,128,128]{3,2,1,0:T(8,128)}, f32[16,4,128,128]{3,2,1,0:T(8,128)S(1)}, u32[]{:S(2)}) copy-start(f32[16,4,128,128]{3,2,1,0:T(8,128)S(1)} %multiply_add_fusion) | copy-start | bytes 12582916
  78.3 4.3 copy-start.3
  102.3 68.6 %all-to-all-start = ((f32[16,4,128,128]{3,1,0,2:T(4,128)}), f32[16,4,128,128]{3,1,0,2:T(4,128)}, u32[]{:S(2)}, u32[]{:S(2)}) async-start(f32[16,4,128,128]{3,1,0,2:T(4,128)} %copy.26), calls=%async_computation | async-start | bytes 8388608 | tf_op jit(solution)/shard_map/all_to_all | solution.py:70
  112.4 6.1 %copy-start.4 = (f32[16,4,128,128]{3,2,1,0:T(8,128)S(1)}, f32[16,4,128,128]{3,2,1,0:T(8,128)}, u32[]{:S(2)}) copy-start(f32[16,4,128,128]{3,2,1,0:T(8,128)} %copy-done.3) | copy-start | bytes 12582916
  170.9 68.2 %all-to-all-start.1 = ((f32[16,4,128,128]{3,1,0,2:T(4,128)}), f32[16,4,128,128]{3,1,0,2:T(4,128)}, u32[]{:S(2)}, u32[]{:S(2)}) async-start(f32[16,4,128,128]{3,1,0,2:T(4,128)} %copy.31), calls=%async_computation.1 | async-start | bytes 8388608 | tf_op jit(solution)/shard_map/all_to_all | solution.py:71
  242.5 4.3 copy-start.6
  256.3 4.8 %copy-start.5 = (f32[128,16,4,128]{3,0,2,1:T(8,128)}, f32[128,16,4,128]{3,0,2,1:T(8,128)S(1)}, u32[]{:S(2)}) copy-start(f32[128,16,4,128]{3,0,2,1:T(8,128)S(1)} %add_multiply_fusion) | copy-start | bytes 12582916
  261.1 4.4 copy-start
  274.9 62.3 %all-to-all-start.2 = ((f32[16,128,4,128]{3,2,0,1:T(4,128)}), f32[16,128,4,128]{3,2,0,1:T(4,128)}, u32[]{:S(2)}, u32[]{:S(2)}) async-start(f32[16,128,4,128]{3,2,0,1:T(4,128)} %copy.38), calls=%async_computation.2 | async-start | bytes 8388608 | tf_op jit(solution)/shard_map/all_to_all | solution.py:79
  283.7 6.1 %copy-start.1 = (f32[128,16,4,128]{3,0,2,1:T(8,128)S(1)}, f32[128,16,4,128]{3,0,2,1:T(8,128)}, u32[]{:S(2)}) copy-start(f32[128,16,4,128]{3,0,2,1:T(8,128)} %copy-done) | copy-start | bytes 12582916
  337.2 65.0 %all-to-all-start.3 = ((f32[16,128,4,128]{3,2,0,1:T(4,128)}), f32[16,128,4,128]{3,2,0,1:T(4,128)}, u32[]{:S(2)}, u32[]{:S(2)}) async-start(f32[16,128,4,128]{3,2,0,1:T(4,128)} %copy.43), calls=%async_computation.3 | async-start | bytes 8388608 | tf_op jit(solution)/shard_map/all_to_all | solution.py:80
  405.6 4.3 copy-start.7
  426.5 4.7 %copy-start.8 = (f32[8,4,128,128]{3,2,1,0:T(8,128)S(1)}, f32[8,4,128,128]{3,2,1,0:T(8,128)}, u32[]{:S(2)}) copy-start(f32[8,4,128,128]{3,2,1,0:T(8,128)} %get-tuple-element.5) | copy-start | bytes 6291460
Sparse Core Ops, SparseCore 0:
  9.0 47.6 all-gather.1
where the time goes:
time: 457 us; the launch traced here: 448 us
  waiting for transfers between devices  233 us (51%)
  matrix products  117 us (26%)
  starting transfers between devices  39.3 us (9%)
  local copies, waits for them, and re-layouts  37.6 us (8%)
  between operations  14.2 us (3%)
  other arithmetic  7.21 us (2%)
    dot_general x24, matrix products, apply(): jnp.einsum(form, values, table, precision=lax.Precision.HIGHEST, preferre...  117 us
    all_to_all x1, waiting for transfers between devices, per_device(): lax.all_to_all(col_imag, 'slab', split_axis=1, concat_axis=2, tiled=True)  52.2 us
    all_to_all x1, waiting for transfers between devices, per_device(): lax.all_to_all(imag_part, 'slab', split_axis=2, concat_axis=1, tiled=True)  49.6 us
    all_gather x1, waiting for transfers between devices, per_device(): source = lax.all_gather(blocks, 'band', axis=0, tiled=True)  48 us
    all_to_all x1, waiting for transfers between devices, per_device(): lax.all_to_all(real_part, 'slab', split_axis=2, concat_axis=1, tiled=True)  43.5 us
    all_to_all x1, waiting for transfers between devices, per_device(): lax.all_to_all(col_real, 'slab', split_axis=1, concat_axis=2, tiled=True)  38.6 us
    all_to_all x1, starting transfers between devices, per_device(): lax.all_to_all(imag_part, 'slab', split_axis=2, concat_axis=1, tiled=True)  13 us
    all_to_all x1, starting transfers between devices, per_device(): lax.all_to_all(real_part, 'slab', split_axis=2, concat_axis=1, tiled=True)  10.1 us
  transfers between devices with their start and end apart: 5, of which 5 were waited for; matrix products, arithmetic and copies ran while one was open for 9% of the time, Pallas kernels for 0%

commit v1 on v0

--- a/solution.py
+++ b/solution.py
@@ -67,7 +67,12 @@
     imag_part = imag_part.reshape(flat)
     all_waves = wave_of(jnp.arange(grid_len, dtype=jnp.int32), grid_len)
     position = lax.axis_index("slab")
-    col_real = lax.all_to_all(real_part, "slab", split_axis=2, concat_axis=1, tiled=True)
+    col_real = jnp.concatenate(
+        lax.all_to_all(
+            jnp.stack(jnp.split(real_part, lax.axis_size("slab"), axis=2)), "slab", 0, 0
+        ),
+        axis=1,
+    )
     col_imag = lax.all_to_all(imag_part, "slab", split_axis=2, concat_axis=1, tiled=True)
     width_y = col_real.shape[2]
     local_waves = wave_of(position * width_y + jnp.arange(width_y, dtype=jnp.int32), grid_len)

time: 457 us -> 456 us (level)
  the two profiles are of different devices: /device:TPU:6 before, /device:TPU:16 now
where the time goes in v1:
time: 456 us; the launch traced here: 447 us
  waiting for transfers between devices  219 us (48%)
  matrix products  114 us (25%)
  local copies, waits for them, and re-layouts  53.7 us (12%)
  starting transfers between devices  39.2 us (9%)
  between operations  14.3 us (3%)
  other arithmetic  7.21 us (2%)
    dot_general x24, matrix products, apply(): jnp.einsum(form, values, table, precision=lax.Precision.HIGHEST, preferre...  114 us
    all_to_all x1, waiting for transfers between devices, per_device(): lax.all_to_all(col_imag, 'slab', split_axis=1, concat_axis=2, tiled=True)  50.6 us
    all_gather x1, waiting for transfers between devices, per_device(): source = lax.all_gather(blocks, 'band', axis=0, tiled=True)  48.5 us
    all_to_all x1, waiting for transfers between devices, per_device(): lax.all_to_all(jnp.stack(jnp.split(real_part, lax.axis_size('slab'), axis...  42.7 us
    all_to_all x1, waiting for transfers between devices, per_device(): lax.all_to_all(col_real, 'slab', split_axis=1, concat_axis=2, tiled=True)  41 us
    all_to_all x1, waiting for transfers between devices, per_device(): lax.all_to_all(imag_part, 'slab', split_axis=2, concat_axis=1, tiled=True)  35.9 us
    unnamed x53, local copies, waits for them, and re-layouts  21.4 us
    all_to_all x1, starting transfers between devices, per_device(): lax.all_to_all(imag_part, 'slab', split_axis=2, concat_axis=1, tiled=True)  15.4 us
  transfers between devices with their start and end apart: 5, of which 5 were waited for; matrix products, arithmetic and copies ran while one was open for 13% of the time, Pallas kernels for 0%

profile of v1, /device:TPU:16, one launch (start us, length us, event | category | flops | bytes accessed | tf_op | source)
XLA Modules:
  0.0 447.4 jit_solution(2688342162333612199)
XLA Ops:
  6.5 0.7 all-gather.2.cloned.1.call-update
  7.3 0.7 slice.17
  8.0 0.7 slice.16
  8.8 48.5 %all-gather.2.cloned.1.call-done = f32[16,4,128,128]{3,2,1,0:T(8,128)} async-done(((f32[4,4,128,128]{3,2,1,0:T(8,128)}), f32[16,4,128,128]{3,2,1,0:T(8,128)}) %all-gather.2.cloned.1.call-update) | async-done | bytes 4194320 | tf_op jit(solution)/shard_map/all_gather | solution.py:50
  57.2 4.7 %multiply_multiply_fusion = (f32[8,4,128,128]{3,2,1,0:T(8,128)}, f32[8,4,128,128]{3,2,1,0:T(8,128)S(1)}, f32[8,4,128,128]{3,2,1,0:T(8,128)S(1)}, f32[8,4,128,128]{3,2,1,0:T(8,128)S(1)}) fusion(f32[8]{0:T(128)S(1)} %slice.17, f32[16,4,128,128]{3,2,1,0:T(8,128)} %all-gather.2.cloned.1.call-done, f32[8]{0:T(128)S(1)} %slice.16), kind=kLoop, calls=%fused_computation.34 | loop fusion | flops 2097152 | bytes 12582976 | tf_op jit(solution)/shard_map/mul | solution.py:95
  62.0 1.4 broadcast_multiply_fusion
  63.4 3.8 fusion.87
  67.2 3.7 fusion.85
  70.8 4.1 multiply_subtract_fusion
  74.9 3.8 multiply_add_fusion
  78.8 4.3 fusion.89
  83.1 4.7 %subtract_bitcast_fusion.1 = f32[16,4,128,128]{3,2,1,0:T(8,128)S(1)} fusion(f32[128,16,4,128]{3,0,2,1:T(8,128)S(1)} %fusion.89, f32[16,4,128,128]{3,2,1,0:T(8,128)S(1)} %multiply_add_fusion), kind=kOutput, calls=%fused_computation.23 | convolution fusion | flops 1612939264 | bytes 12582912 | tf_op jit(solution)/shard_map/fzyx,yk->fzkx/dot_general | solution.py:20
  88.5 0.7 fusion.60
  89.9 0.7 fusion.58
  90.6 0.7 fusion.57
  92.6 0.7 fusion.54
  94.0 0.7 fusion.52
  94.7 0.7 fusion.51
  95.4 0.7 fusion.50
  96.1 0.7 fusion.49
  97.5 0.7 fusion.47
  98.2 0.7 fusion.46
  98.9 0.7 fusion.45
  100.3 0.7 fusion.43
  101.6 0.7 fusion.41
  102.3 0.7 fusion.40
  104.4 0.7 fusion.37
  105.7 0.7 fusion.35
  107.8 0.7 fusion.32
  108.5 0.7 fusion.31
  109.9 9.7 %all-to-all-start = ((f32[32,16,4,4,128]{4,3,2,1,0:T(4,128)}), f32[32,16,4,4,128]{4,3,2,1,0:T(4,128)}, u32[]{:S(2)}, u32[]{:S(2)}) async-start(f32[32,16,4,4,128]{4,3,2,1,0:T(4,128)} %fusion.30), calls=%async_computation | async-start | bytes 8388608 | tf_op jit(solution)/shard_map/all_to_all | solution.py:71
  119.6 6.1 %fusion.81 = f32[128,16,4,128]{3,0,2,1:T(8,128)S(1)} fusion(f32[16,4,128,128]{3,2,1,0:T(8,128)} %copy-done.4), kind=kOutput, calls=%fused_computation.126 | convolution fusion | flops 1610842112 | bytes 8388608 | tf_op jit(solution)/shard_map/fzyx,yk->fzkx/dot_general | solution.py:20
  125.7 4.3 add_bitcast_fusion.1
  130.0 4.7 %copy.52 = f32[16,4,128,128]{3,1,0,2:T(4,128)} copy(f32[16,4,128,128]{3,2,1,0:T(8,128)S(1)} %add_bitcast_fusion.1) | data formatting | bytes 8388608 | tf_op jit(solution)/shard_map/add | solution.py:28
  134.7 42.7 %all-to-all-done = f32[32,16,4,4,128]{4,3,2,1,0:T(4,128)} async-done(((f32[32,16,4,4,128]{4,3,2,1,0:T(4,128)}), f32[32,16,4,4,128]{4,3,2,1,0:T(4,128)}, u32[]{:S(2)}, u32[]{:S(2)}) %all-to-all-start) | async-done | bytes 4194336 | tf_op jit(solution)/shard_map/all_to_all | solution.py:71
  177.4 15.4 %all-to-all-start.1 = ((f32[16,4,128,128]{3,1,0,2:T(4,128)}), f32[16,4,128,128]{3,1,0,2:T(4,128)}, u32[]{:S(2)}, u32[]{:S(2)}) async-start(f32[16,4,128,128]{3,1,0,2:T(4,128)} %copy.52), calls=%async_computation.1 | async-start | bytes 8388608 | tf_op jit(solution)/shard_map/all_to_all | solution.py:76
  193.0 3.9 copy.47
  197.0 7.8 %fusion.16 = f32[128,16,4,128]{3,0,2,1:T(8,128)} fusion(f32[16,128,4,128]{3,0,2,1:T(8,128)S(1)} %bitcast.286), kind=kOutput, calls=%fused_computation.26 | convolution fusion | flops 1610842112 | bytes 8388608 | tf_op jit(solution)/shard_map/fzyx,zk->fkyx/dot_general | solution.py:20
  204.7 7.9 %fusion.18 = f32[128,16,4,128]{3,0,2,1:T(8,128)} fusion(f32[16,128,4,128]{3,0,2,1:T(8,128)S(1)} %bitcast.287), kind=kOutput, calls=%fused_computation.28 | convolution fusion | flops 1610842112 | bytes 8388608 | tf_op jit(solution)/shard_map/fzyx,zk->fkyx/dot_general | solution.py:20
  212.6 35.9 %all-to-all-done.1 = f32[16,4,128,128]{3,1,0,2:T(4,128)} async-done(((f32[16,4,128,128]{3,1,0,2:T(4,128)}), f32[16,4,128,128]{3,1,0,2:T(4,128)}, u32[]{:S(2)}, u32[]{:S(2)}) %all-to-all-start.1) | async-done | bytes 4194336 | tf_op jit(solution)/shard_map/all_to_all | solution.py:76
  248.5 3.5 copy.53
  252.1 5.2 %add_multiply_fusion = f32[128,16,4,128]{3,0,2,1:T(8,128)S(1)} fusion(f32[128,16,4,128]{3,0,2,1:T(8,128)S(1)} %copy-done.8, f32[16,128,4,128]{3,1,2,0:T(8,128)S(1)} %bitcast.280, f32[128,4,128]{2,0,1:T(8,128)S(1)} %add_divide_fusion), kind=kOutput, calls=%fused_computation.20 | convolution fusion | flops 1613987840 | bytes 12845056 | tf_op jit(solution)/shard_map/fzyx,zk->fkyx/dot_general | solution.py:20
  257.2 4.8 %subtract_multiply_fusion = f32[128,16,4,128]{3,0,2,1:T(8,128)S(1)} fusion(f32[128,16,4,128]{3,0,2,1:T(8,128)S(1)} %copy-done.7, f32[16,128,4,128]{3,1,2,0:T(8,128)S(1)} %bitcast.281, f32[128,4,128]{2,0,1:T(8,128)S(1)} %add_divide_fusion), kind=kOutput, calls=%fused_computation.21 | convolution fusion | flops 1613987840 | bytes 12845056 | tf_op jit(solution)/shard_map/fzyx,zk->fkyx/dot_general | solution.py:20
  262.0 4.6 %fusion.10 = f32[128,16,4,128]{3,0,2,1:T(8,128)S(1)} fusion(f32[128,16,4,128]{3,0,2,1:T(8,128)S(1)} %add_multiply_fusion), kind=kOutput, calls=%fused_computation.10 | convolution fusion | flops 1610842112 | bytes 8388608 | tf_op jit(solution)/shard_map/fzyx,zk->fkyx/dot_general | solution.py:20
  266.6 4.3 subtract_bitcast_fusion
  271.0 4.7 %copy.60 = f32[16,128,4,128]{3,2,0,1:T(4,128)} copy(f32[16,128,4,128]{3,1,2,0:T(8,128)S(1)} %subtract_bitcast_fusion) | data formatting | bytes 8388608 | tf_op jit(solution)/shard_map/sub | solution.py:28
  275.6 7.4 %all-to-all-start.2 = ((f32[16,128,4,128]{3,2,0,1:T(4,128)}), f32[16,128,4,128]{3,2,0,1:T(4,128)}, u32[]{:S(2)}, u32[]{:S(2)}) async-start(f32[16,128,4,128]{3,2,0,1:T(4,128)} %copy.60), calls=%async_computation.2 | async-start | bytes 8388608 | tf_op jit(solution)/shard_map/all_to_all | solution.py:84
  283.0 6.1 %fusion.8 = f32[128,16,4,128]{3,0,2,1:T(8,128)S(1)} fusion(f32[128,16,4,128]{3,0,2,1:T(8,128)} %copy-done.5), kind=kOutput, calls=%fused_computation.8 | convolution fusion | flops 1610842112 | bytes 8388608 | tf_op jit(solution)/shard_map/fzyx,zk->fkyx/dot_general | solution.py:20
  289.1 4.1 add_bitcast_fusion
  293.2 4.7 %copy.65 = f32[16,128,4,128]{3,2,0,1:T(4,128)} copy(f32[16,128,4,128]{3,1,2,0:T(8,128)S(1)} %add_bitcast_fusion) | data formatting | bytes 8388608 | tf_op jit(solution)/shard_map/add | solution.py:28
  297.8 41.0 %all-to-all-done.2 = f32[16,128,4,128]{3,2,0,1:T(4,128)} async-done(((f32[16,128,4,128]{3,2,0,1:T(4,128)}), f32[16,128,4,128]{3,2,0,1:T(4,128)}, u32[]{:S(2)}, u32[]{:S(2)}) %all-to-all-start.2) | async-done | bytes 4194336 | tf_op jit(solution)/shard_map/all_to_all | solution.py:84
  338.9 6.7 %all-to-all-start.3 = ((f32[16,128,4,128]{3,2,0,1:T(4,128)}), f32[16,128,4,128]{3,2,0,1:T(4,128)}, u32[]{:S(2)}, u32[]{:S(2)}) async-start(f32[16,128,4,128]{3,2,0,1:T(4,128)} %copy.65), calls=%async_computation.3 | async-start | bytes 8388608 | tf_op jit(solution)/shard_map/all_to_all | solution.py:85
  345.6 5.3 %copy.61 = f32[16,32,4,4,128]{4,3,1,2,0:T(4,128)} copy(f32[16,32,4,4,128]{4,3,0,2,1:T(4,128)} %bitcast.62) | data formatting | bytes 8388608 | tf_op jit(solution)/shard_map/all_to_all | solution.py:84
  350.9 50.6 %all-to-all-done.3 = f32[16,128,4,128]{3,2,0,1:T(4,128)} async-done(((f32[16,128,4,128]{3,2,0,1:T(4,128)}), f32[16,128,4,128]{3,2,0,1:T(4,128)}, u32[]{:S(2)}, u32[]{:S(2)}) %all-to-all-start.3) | async-done | bytes 4194336 | tf_op jit(solution)/shard_map/all_to_all | solution.py:85
  401.5 3.4 copy.66
  404.8 4.3 fusion.77
  409.2 4.3 fusion.93
  413.5 4.6 %convolution_add_fusion = f32[128,16,4,128]{3,0,2,1:T(8,128)S(1)} fusion(f32[128,16,4,128]{3,0,2,1:T(8,128)S(1)} %fusion.77, f32[16,4,128,128]{3,2,1,0:T(8,128)S(1)} %bitcast.283), kind=kOutput, calls=%fused_computation.32 | convolution fusion | flops 1611890688 | bytes 12582912 | tf_op jit(solution)/shard_map/fzyx,yk->fzkx/dot_general | solution.py:20
  418.1 3.8 fusion
  421.9 3.8 fusion.2
  425.7 4.7 %convolution_subtract_fusion = f32[128,16,4,128]{3,0,2,1:T(8,128)S(1)} fusion(f32[128,16,4,128]{3,0,2,1:T(8,128)S(1)} %fusion.93, f32[16,4,128,128]{3,2,1,0:T(8,128)S(1)} %bitcast.285), kind=kOutput, calls=%fused_computation.33 | convolution fusion | flops 1611890688 | bytes 12582912 | tf_op jit(solution)/shard_map/fzyx,yk->fzkx/dot_general | solution.py:20
  430.5 4.4 multiply_reduce_fusion
  434.8 4.4 multiply_reduce_fusion.1
  439.2 0.9 add_negate_fusion
  (41 shorter events, 9.8 us)
Async XLA Ops:
  6.5 50.7 %all-gather.2.cloned.1.call-start = ((), (), s32[]{:S(2)}) async-start(), calls=%async_computation.4 | async-start | bytes 5242880 | tf_op jit(solution)/shard_map/all_gather | solution.py:50
  8.7 53.2 %copy-start.10 = (f32[2,4,128,128]{3,2,1,0:T(8,128)S(1)}, f32[2,4,128,128]{3,2,1,0:T(8,128)}, u32[]{:S(2)}) copy-start(f32[2,4,128,128]{3,2,1,0:T(8,128)} %param.3) | copy-start | bytes 1572868
  74.9 3.8 copy-start.2
  78.7 4.3 copy-start.4
  109.9 67.5 %all-to-all-start = ((f32[32,16,4,4,128]{4,3,2,1,0:T(4,128)}), f32[32,16,4,4,128]{4,3,2,1,0:T(4,128)}, u32[]{:S(2)}, u32[]{:S(2)}) async-start(f32[32,16,4,4,128]{4,3,2,1,0:T(4,128)} %fusion.30), calls=%async_computation | async-start | bytes 8388608 | tf_op jit(solution)/shard_map/all_to_all | solution.py:71
  119.6 6.1 %copy-start.3 = (f32[16,4,128,128]{3,2,1,0:T(8,128)S(1)}, f32[16,4,128,128]{3,2,1,0:T(8,128)}, u32[]{:S(2)}) copy-start(f32[16,4,128,128]{3,2,1,0:T(8,128)} %copy-done.2) | copy-start | bytes 12582916
  177.4 71.1 %all-to-all-start.1 = ((f32[16,4,128,128]{3,1,0,2:T(4,128)}), f32[16,4,128,128]{3,1,0,2:T(4,128)}, u32[]{:S(2)}, u32[]{:S(2)}) async-start(f32[16,4,128,128]{3,1,0,2:T(4,128)} %copy.52), calls=%async_computation.1 | async-start | bytes 8388608 | tf_op jit(solution)/shard_map/all_to_all | solution.py:76
  248.5 3.5 copy-start.8
  252.0 5.2 %copy-start.7 = (f32[128,16,4,128]{3,0,2,1:T(8,128)S(1)}, f32[128,16,4,128]{3,0,2,1:T(8,128)}, u32[]{:S(2)}) copy-start(f32[128,16,4,128]{3,0,2,1:T(8,128)} %fusion.18) | copy-start | bytes 12582916
  257.2 4.8 %copy-start.5 = (f32[128,16,4,128]{3,0,2,1:T(8,128)}, f32[128,16,4,128]{3,0,2,1:T(8,128)S(1)}, u32[]{:S(2)}) copy-start(f32[128,16,4,128]{3,0,2,1:T(8,128)S(1)} %add_multiply_fusion) | copy-start | bytes 12582916
  262.0 4.6 %copy-start = (f32[128,16,4,128]{3,0,2,1:T(8,128)}, f32[128,16,4,128]{3,0,2,1:T(8,128)S(1)}, u32[]{:S(2)}) copy-start(f32[128,16,4,128]{3,0,2,1:T(8,128)S(1)} %subtract_multiply_fusion) | copy-start | bytes 12582916
  275.6 63.3 %all-to-all-start.2 = ((f32[16,128,4,128]{3,2,0,1:T(4,128)}), f32[16,128,4,128]{3,2,0,1:T(4,128)}, u32[]{:S(2)}, u32[]{:S(2)}) async-start(f32[16,128,4,128]{3,2,0,1:T(4,128)} %copy.60), calls=%async_computation.2 | async-start | bytes 8388608 | tf_op jit(solution)/shard_map/all_to_all | solution.py:84
  283.0 6.1 %copy-start.1 = (f32[128,16,4,128]{3,0,2,1:T(8,128)S(1)}, f32[128,16,4,128]{3,0,2,1:T(8,128)}, u32[]{:S(2)}) copy-start(f32[128,16,4,128]{3,0,2,1:T(8,128)} %copy-done) | copy-start | bytes 12582916
  338.9 62.6 %all-to-all-start.3 = ((f32[16,128,4,128]{3,2,0,1:T(4,128)}), f32[16,128,4,128]{3,2,0,1:T(4,128)}, u32[]{:S(2)}, u32[]{:S(2)}) async-start(f32[16,128,4,128]{3,2,0,1:T(4,128)} %copy.65), calls=%async_computation.3 | async-start | bytes 8388608 | tf_op jit(solution)/shard_map/all_to_all | solution.py:85
  404.8 4.3 copy-start.6
  425.7 4.7 %copy-start.9 = (f32[8,4,128,128]{3,2,1,0:T(8,128)S(1)}, f32[8,4,128,128]{3,2,1,0:T(8,128)}, u32[]{:S(2)}) copy-start(f32[8,4,128,128]{3,2,1,0:T(8,128)} %get-tuple-element.5) | copy-start | bytes 6291460
Sparse Core Ops, SparseCore 0:
  9.0 48.1 all-gather.1
